TPU v7x, 256 devices: a whole 4x4x8 slice. The times are simulated.
256 devices in a mesh: row: 64 (over z, x, core), rep: 4 (over y).
Axes of the slice: x: 4, y: 4, z: 8, core: 2. Of those that a mesh axis runs over, the one named last changes fastest.
Arguments:
- features: bfloat16 [32768, 256], P(('row', 'rep')), may hold values from -6 to 6
- weight: bfloat16 [256, 256], replicated, may hold values from -0.375 to 0.375
- bias: float32 [256], replicated, may hold values from -3 to 3
- cotangent: bfloat16 [32768, 256], P(('row', 'rep')), may hold values from -6 to 6
- tile_values: bfloat16 [64, 4, 192, 128, 128], P('row', 'rep')
- tile_rows: int32 [64, 4, 192], P('row', 'rep'), may hold values from 0 to 3, as said below
- tile_cols: int32 [64, 4, 192], P('row', 'rep'), may hold values from 0 to 63, as said below
- tile_count: int32 [64, 4], P('row', 'rep'), may hold values from 1 to 192, as said below
Outputs:
- activation: bfloat16 [32768, 256], P(('row', 'rep'))
- grad_features: bfloat16 [32768, 256], P(('row', 'rep'))
- grad_weight: float32 [256, 256], replicated
- grad_bias: float32 [256], replicated
Inputs may be any that keep to these rules, and one draw needn't show every extreme that they name: `tile_rows`: tile row of a slot, below 4; the (row, column) pairs of the 192 slots of one row block and column group are distinct. `tile_cols`: tile column of a slot within its column group. `tile_count`: slots at or past the count hold arbitrary values and are ignored; some row block and column group fills all 192 slots.
All inputs are finite; a program needn't handle non-finite values.
Results may differ from a plain program's by a relative error of at most 0.0075.
Values may be sent and summed in bfloat16 or wider, within the bound.
A program may use at most 128 MiB of HBM per device.

v0:
```python
import jax
import jax.numpy as jnp
from jax import lax
from jax.sharding import PartitionSpec as P


def silu_parts(pre):
    sig = jax.nn.sigmoid(pre)
    return (pre * sig, sig * (1.0 + pre * (1.0 - sig)))


def on_device(features, weight, bias, cotangent, tile_values, tile_rows, tile_cols, tile_count):
    highest = lax.Precision.HIGHEST
    node_rows, feat = features.shape
    values = tile_values[0, 0]
    rows = tile_rows[0, 0]
    cols = tile_cols[0, 0]
    slots = values.shape[0]
    tile = values.shape[-1]
    groups = lax.axis_size("rep")
    blocks = lax.axis_size("row")
    block_rows = groups * node_rows
    trows = block_rows // tile
    tcols = blocks * node_rows // tile
    alive = (jnp.arange(slots, dtype=jnp.int32) < tile_count[0, 0]).astype(jnp.float32)
    xw = jnp.dot(features, weight, preferred_element_type=jnp.float32).astype(jnp.bfloat16)
    gathered = lax.all_gather(xw, "row", axis=0, tiled=True)
    taken = gathered.reshape(tcols, tile, feat)[cols]
    prod = jnp.einsum("kab,kbf->kaf", values, taken, preferred_element_type=jnp.float32)
    onehot = (rows[:, None] == jnp.arange(trows, dtype=jnp.int32)[None, :]).astype(
        jnp.float32
    ) * alive[:, None]
    partial_value = jnp.einsum("kr,kaf->raf", onehot, prod, precision=highest).reshape(
        block_rows, feat
    )
    pre = lax.psum_scatter(partial_value, "rep", scatter_dimension=0, tiled=True) + bias[None, :]
    output, slope = silu_parts(pre)
    dpre = (cotangent.astype(jnp.float32) * slope).astype(jnp.bfloat16)
    dblock = lax.all_gather(dpre, "rep", axis=0, tiled=True)
    activation = output.astype(jnp.bfloat16)
    dtaken = dblock.reshape(trows, tile, feat)[rows]
    back_prod = jnp.einsum("kab,kaf->kbf", values, dtaken, preferred_element_type=jnp.float32)
    back_prod = back_prod * alive[:, None, None]
    terms = jax.ops.segment_sum(back_prod, cols, num_segments=tcols).reshape(tcols * tile, feat)
    back = lax.psum_scatter(terms, "row", scatter_dimension=0, tiled=True)
    back_b = back.astype(jnp.bfloat16)
    grad_features = lax.dot_general(
        back_b, weight, (((1,), (1,)), ((), ())), preferred_element_type=jnp.float32
    ).astype(jnp.bfloat16)
    weight_term = lax.dot_general(
        features, back_b, (((0,), (0,)), ((), ())), preferred_element_type=jnp.float32
    )
    bias_term = jnp.sum(dpre.astype(jnp.float32), axis=0)
    weight_total, bias_total = lax.psum((weight_term, bias_term), ("row", "rep"))
    scale = 1.0 / jnp.sqrt(jnp.float32(node_rows * blocks * groups))
    return (activation, grad_features, weight_total * scale, bias_total * scale)


def solution(mesh):
    in_specs = (
        P(("row", "rep"), None),
        P(),
        P(),
        P(("row", "rep"), None),
        P("row", "rep", None, None, None),
        P("row", "rep", None),
        P("row", "rep", None),
        P("row", "rep"),
    )
    out_specs = (P(("row", "rep"), None), P(("row", "rep"), None), P(), P())
    return jax.shard_map(
        on_device, mesh=mesh, in_specs=in_specs, out_specs=out_specs, check_vma=False
    )
```

profile of v0, /device:TPU:1, one launch (start us, length us, event | category | flops | bytes accessed | tf_op | source)
XLA Modules:
  0.0 718.6 jit_solution(18022359150745797858)
XLA Ops:
  7.2 0.8 copy-done
  8.1 1.6 convolution_convert_fusion.1
  10.4 0.7 compare_select_fusion.1
  11.1 83.4 %all-gather.2.cloned.1.call-done = bf16[8192,256]{1,0:T(8,128)(2,1)} async-done(((bf16[128,256]{1,0:T(8,128)(2,1)}), bf16[8192,256]{1,0:T(8,128)(2,1)}) %all-gather.2.cloned.1.call-update) | async-done | bytes 4194320 | tf_op jit(solution)/shard_map/all_gather | solution.py:27
  94.6 10.5 %gather_fusion = bf16[192,128,256]{2,1,0:T(8,128)(2,1)} fusion(bf16[64,128,256]{2,1,0:T(8,128)(2,1)} %bitcast.37, s32[1024]{0:T(1024)S(1)} %pad_clamp_fusion.1), kind=kCustom, calls=%fused_computation | custom fusion | bytes 25166592 | tf_op jit(solution)/shard_map/gather | solution.py:28
  105.0 13.8 %fusion.3 = f32[192,256,128]{2,1,0:T(8,128)} fusion(bf16[192,128,256]{2,1,0:T(8,128)(2,1)} %gather_fusion, bf16[1,1,192,128,128]{4,3,2,1,0:T(8,128)(2,1)} %param.12), kind=kOutput, calls=%fused_computation.7 | convolution fusion | flops 1610612736 | bytes 44040192 | tf_op jit(solution)/shard_map/kab,kbf->kaf/dot_general | solution.py:29
  118.8 24.8 %copy.18 = f32[192,256,128]{1,0,2:T(8,128)} copy(f32[192,256,128]{2,1,0:T(8,128)} %fusion.3) | data formatting | bytes 50331648 | tf_op jit(solution)/shard_map/kab,kbf->kaf/dot_general | solution.py:29
  143.6 15.6 %fusion = f32[4,128,256]{2,0,1:T(4,128)S(1)} fusion(f32[192,256,128]{1,0,2:T(8,128)} %copy.18, f32[192]{0:T(256)S(1)} %compare_convert_fusion, s32[192]{0:T(256)S(1)} %bitcast.39), kind=kOutput, calls=%fused_computation.3 | convolution fusion | flops 301991424 | bytes 25691648 | tf_op jit(solution)/shard_map/kr,kaf->raf/dot_general | solution.py:33
  159.2 0.9 copy.14
  160.2 19.3 %reduce-scatter.3.cloned.1.call-done = f32[128,256]{1,0:T(8,128)} async-done(((f32[512,256]{1,0:T(8,128)}), f32[128,256]{1,0:T(8,128)}) %reduce-scatter.3.cloned.1.call-update) | async-done | bytes 131088 | tf_op jit(solution)/shard_map/reduce_scatter | solution.py:36
  179.5 1.6 convert_reduce_fusion
  181.1 9.9 %all_gather.7 = bf16[512,256]{1,0:T(8,128)(2,1)S(1)} all-gather(bf16[128,256]{1,0:T(8,128)(2,1)S(1)} %get-tuple-element.13), channel_id=1, replica_groups=mesh['row'=64,'rep'=4] {'rep'}, dimensions={0}, use_global_device_ids=true | all-gather | bytes 327680 | tf_op jit(solution)/shard_map/all_gather | solution.py:39
  191.0 8.1 %gather_fusion.1 = bf16[192,128,256]{2,1,0:T(8,128)(2,1)} fusion(bf16[4,128,256]{2,1,0:T(8,128)(2,1)S(1)} %bitcast.35, s32[1024]{0:T(1024)S(1)} %pad_clamp_fusion), kind=kCustom, calls=%fused_computation.1 | custom fusion | bytes 25166592 | tf_op jit(solution)/shard_map/gather | solution.py:41
  199.0 15.8 %multiply_bitcast_fusion = f32[192,128,256]{1,2,0:T(8,128)} fusion(f32[192]{0:T(256)S(1)} %compare_convert_fusion, bf16[192,128,256]{2,1,0:T(8,128)(2,1)} %gather_fusion.1, bf16[1,1,192,128,128]{4,3,2,1,0:T(8,128)(2,1)} %param.12), kind=kOutput, calls=%fused_computation.5 | convolution fusion | flops 1616904192 | bytes 44040960 | tf_op jit(solution)/shard_map/kab,kaf->kbf/dot_general | solution.py:42
  214.8 24.7 %copy.16 = f32[192,128,256]{2,1,0:T(8,128)} copy(f32[192,128,256]{1,2,0:T(8,128)} %multiply_bitcast_fusion) | data formatting | bytes 50331648 | tf_op jit(solution)/shard_map/mul | solution.py:43
  239.5 4.2 broadcast_in_dim.2
  243.7 57.6 %scatter_fusion = f32[64,128,256]{2,1,0:T(8,128)} fusion(f32[64,128,256]{2,1,0:T(8,128)} %broadcast_in_dim.2, s32[192]{0:T(256)S(1)} %bitcast.40, f32[192,128,256]{2,1,0:T(8,128)} %copy.16), kind=kCustom, calls=%fused_computation.2 | custom fusion | flops 6291456 | bytes 75498240 | tf_op jit(solution)/shard_map/scatter-add | solution.py:44
  301.4 80.0 %psum.15 = f32[256]{0:T(256)S(1)} all-reduce(f32[256]{0:T(256)S(1)} %get-tuple-element.12), channel_id=1, replica_groups=mesh['row'=64,'rep'=4] {'row','rep'}, use_global_device_ids=true, to_apply=%region_5.0 | all-reduce | flops 256 | bytes 2048 | tf_op jit(solution)/shard_map/psum | solution.py:54
  382.0 69.6 %reduce-scatter.5.cloned.1.call-done = f32[128,256]{1,0:T(8,128)} async-done(((f32[8192,256]{1,0:T(8,128)}), f32[128,256]{1,0:T(8,128)}) %reduce-scatter.5.cloned.1.call-update) | async-done | bytes 131088 | tf_op jit(solution)/shard_map/reduce_scatter | solution.py:45
  451.6 1.8 convolution_bitcast_fusion
  453.5 1.7 convolution_convert_fusion
  455.2 255.1 %all-reduce.2.cloned.1.call-done = f32[256,256]{0,1:T(8,128)} async-done(((f32[256,256]{0,1:T(8,128)}), f32[256,256]{0,1:T(8,128)}) %all-reduce.2.cloned.1.call-update) | async-done | bytes 262160 | tf_op jit(solution)/shard_map/psum | solution.py:54
  710.3 1.0 broadcast_multiply_fusion
  711.3 0.8 copy.17
  (24 shorter events, 0.8 us)
Async XLA Ops:
  7.2 0.9 copy-start
  7.2 87.4 %all-gather.2.cloned.1.call-start = ((), (), s32[]{:S(2)}) async-start(), calls=%async_computation.2 | async-start | bytes 4259840 | tf_op jit(solution)/shard_map/all_gather | solution.py:27
  9.7 169.7 %reduce-scatter.3.cloned.1.call-start = ((), (), s32[]{:S(2)}) async-start(), calls=%async_computation.3 | async-start | bytes 655360 | tf_op jit(solution)/shard_map/reduce_scatter | solution.py:36
  118.8 24.8 %copy-start.3 = (s32[1,1,192]{2,1,0:T(1,128)S(1)}, s32[1,1,192]{2,1,0:T(1,128)}, u32[]{:S(2)}) copy-start(s32[1,1,192]{2,1,0:T(1,128)} %param.13) | copy-start | bytes 2308
  143.6 35.8 %copy-start.2 = (bf16[128,256]{1,0:T(8,128)(2,1)S(1)}, bf16[128,256]{1,0:T(8,128)(2,1)}, u32[]{:S(2)}) copy-start(bf16[128,256]{1,0:T(8,128)(2,1)} %param.11) | copy-start | bytes 196612
  143.6 35.8 %copy-start.5 = (f32[256]{0:T(256)S(1)}, f32[256]{0:T(256)}, u32[]{:S(2)}) copy-start(f32[256]{0:T(256)} %param.10) | copy-start | bytes 3076
  160.1 291.5 %reduce-scatter.5.cloned.1.call-start = ((), (), s32[]{:S(2)}) async-start(), calls=%async_computation.4 | async-start | bytes 8519680 | tf_op jit(solution)/shard_map/reduce_scatter | solution.py:45
  214.8 28.9 %copy-start.4 = (s32[1,1,192]{2,1,0:T(1,128)S(1)}, s32[1,1,192]{2,1,0:T(1,128)}, u32[]{:S(2)}) copy-start(s32[1,1,192]{2,1,0:T(1,128)} %param.14) | copy-start | bytes 2308
  243.7 207.9 %copy-start.1 = (bf16[128,256]{1,0:T(8,128)(2,1)S(1)}, bf16[128,256]{1,0:T(8,128)(2,1)}, u32[]{:S(2)}) copy-start(bf16[128,256]{1,0:T(8,128)(2,1)} %param.8) | copy-start | bytes 196612
  301.3 408.9 %all-reduce.2.cloned.1.call-start = ((), (), s32[]{:S(2)}) async-start(), calls=%async_computation.5 | async-start | bytes 524288 | tf_op jit(solution)/shard_map/psum | solution.py:54
Sparse Core Ops, SparseCore 0:
  11.4 83.1 all-gather.1
  160.2 19.2 reduce-scatter.2
  301.5 150.1 reduce-scatter.4
  458.4 251.8 all-reduce.1
where the time goes:
time: 720 us; the launch traced here: 719 us
  waiting for transfers between devices  427 us (59%)
  blocking collectives  89.9 us (12%)
  local copies, waits for them, and re-layouts  74.8 us (10%)
  other arithmetic  61.5 us (9%)
  matrix products  50.3 us (7%)
  between operations  14.5 us (2%)
    psum x1, waiting for transfers between devices, on_device(): lax.psum((weight_term, bias_term), ('row', 'rep'))  255 us
    all_gather x1, waiting for transfers between devices, on_device(): gathered = lax.all_gather(xw, 'row', axis=0, tiled=True)  83.4 us
    psum x1, blocking collectives, on_device(): lax.psum((weight_term, bias_term), ('row', 'rep'))  80 us
    reduce_scatter x1, waiting for transfers between devices, on_device(): back = lax.psum_scatter(terms, 'row', scatter_dimension=0, tiled=True)  69.6 us
    scatter-add x1, other arithmetic, on_device(): jax.ops.segment_sum(back_prod, cols, num_segments=tcols)  57.6 us
    dot_general x1, local copies, waits for them, and re-layouts, on_device(): jnp.einsum('kab,kbf->kaf', values, taken, preferred_element_type=jnp.floa...  24.8 us
    mul x1, local copies, waits for them, and re-layouts, on_device(): back_prod = back_prod * alive[:, None, None]  24.7 us
    reduce_scatter x1, waiting for transfers between devices, on_device(): lax.psum_scatter(partial_value, 'rep', scatter_dimension=0, tiled=True)  19.3 us
  transfers between devices with their start and end apart: 4, of which 4 were waited for; matrix products, arithmetic and copies ran while one was open for 0% of the time, Pallas kernels for 0%

commit v1 on v0

v1 whole, which is shorter than its diff:
```python
import functools

import jax
import jax.numpy as jnp
from jax import lax
from jax.experimental import pallas as pl
from jax.experimental.pallas import tpu as pltpu
from jax.sharding import PartitionSpec as P

MESH = pl.DeviceIdType.MESH
F32 = jnp.float32
BF16 = jnp.bfloat16
NZ, NX, NY = 8, 4, 4
DZ = (0, 1, -1, 2, -2, 3, -3, 4)
DX = (0, 1, -1, 2)
GZ = ((0, 1), (1, 3), (3, 5), (5, 7), (7, 8))
GX = ((0, 1), (1, 3), (3, 4))
DIAGS = tuple(
    tuple((a, n - a) for a in range(4, -1, -1) if 0 <= n - a <= 2) for n in range(7)
)


def body(
    tile, slots, cut_rows, cut_feat, scale,
    features, weight, bias, cotangent, values_hbm, rows, cols, count,
    act_out, gf_out, gw_out, gb_out,
    values, inverse_v, inverse, gathered, acc, ysend, yrecv, dt,
    own32, own, sibsend, sibrecv, from_z, from_x,
    g1s, g1r, g2s, g2r, g3s, g3r, g4r, g5, g6, g7,
    send_sem, recv_sem, local_sem,
):
    r = lax.axis_index("row")
    y = lax.axis_index("rep")
    z = r // (2 * NX)
    x = (r // 2) % NX
    k = r % 2
    node_rows, feat = features.shape

    def at(zz, xx, kk, yy):
        return ((zz * NX + xx) * 2 + kk, yy)

    def z_off(d):
        return at((z + d + NZ) % NZ, x, k, y)

    def x_off(d):
        return at(z, (x + d + NX) % NX, k, y)

    def y_off(d):
        return at(z, x, k, (y + d + NY) % NY)

    sibling = at(z, x, 1 - k, y)
    z_far = at((z + 1 - 2 * k + NZ) % NZ, x, k, y)
    x_far = at(z, (x + 1 - 2 * k + NX) % NX, k, y)

    names = {}
    started = []

    def copy(name, src, dst, device):
        i = names.setdefault(name, len(names))
        return pltpu.make_async_remote_copy(
            src_ref=src, dst_ref=dst, send_sem=send_sem.at[i], recv_sem=recv_sem.at[i],
            device_id=device, device_id_type=MESH,
        )

    def send(name, src, dst, device):
        c = copy(name, src, dst, device)
        c.start()
        started.append(c)

    def arrived(name, dst):
        copy(name, dst, dst, sibling).wait_recv()

    tiles_in = pltpu.make_async_copy(
        values_hbm.at[0, 0], values.at[pl.ds(0, slots)], local_sem.at[0]
    )
    tiles_in.start()
    gathered[0, 0, 0] = features[...]
    barrier = pltpu.get_barrier_semaphore()
    peers = (
        [z_off(d) for d in range(1, NZ)]
        + [x_off(d) for d in range(1, NX)]
        + [y_off(d) for d in range(1, NY)]
        + [sibling]
    )
    for p in peers:
        pl.semaphore_signal(barrier, inc=1, device_id=p, device_id_type=MESH)
    pl.semaphore_wait(barrier, len(peers))

    part1 = pl.ds(0, cut_rows)
    part2 = pl.ds(cut_rows, node_rows - cut_rows)
    whole = pl.ds(0, node_rows)

    def span(pair):
        return pl.ds(pair[0], pair[1] - pair[0])

    def ag_z(a, b):
        part = whole if b == 0 else part2
        xs = span(GX[b])
        if a == 0:
            moves = ((0, 1, z_off(1)), (0, 2, z_off(-1)))
        elif a < 3:
            moves = ((2 * a - 1, 2 * a + 1, z_off(1)), (2 * a, 2 * a + 2, z_off(-1)))
        else:
            moves = ((5 + k, 7, z_far),)
        for n, (src, dst, dev) in enumerate(moves):
            send(("agz", a + 1, b, n), gathered.at[src, xs, 0, part], gathered.at[dst, xs, 0, part], dev)

    def ag_z_arrived(a, b):
        part = whole if b == 0 else part2
        for n, s in enumerate(range(*GZ[a])):
            arrived(("agz", a, b, n), gathered.at[s, span(GX[b]), 0, part])

    def ag_x(a, b):
        part = whole if a == 0 else part1
        zs = span(GZ[a])
        moves = ((0, 1, x_off(1)), (0, 2, x_off(-1))) if b == 0 else ((1 + k, 3, x_far),)
        for n, (src, dst, dev) in enumerate(moves):
            send(("agx", a, b + 1, n), gathered.at[zs, src, 0, part], gathered.at[zs, dst, 0, part], dev)

    def ag_x_arrived(a, b):
        part = whole if a == 0 else part1
        for n, s in enumerate(range(*GX[b])):
            arrived(("agx", a, b, n), gathered.at[span(GZ[a]), s, 0, part])

    def ag_pass(a, b):
        if a > 0:
            ag_z_arrived(a, b)
        if b > 0:
            ag_x_arrived(a, b)
        if a < 4:
            ag_z(a, b)
        if b < 2:
            ag_x(a, b)
        zs, xs = span(GZ[a]), span(GX[b])
        send(("ags", a, b), gathered.at[zs, xs, 0], gathered.at[zs, xs, 1], sibling)

    def offset_of(slot):
        half = (slot + 1) // 2
        return half * (2 * (slot % 2) - 1)

    def tile_of(tr, tc):
        p = tr * (NZ * NX * 2) + tc
        return values[inverse[p // 128, p % 128]]

    def tile_pair(tr, tc_own):
        other = tc_own + 1 - 2 * k
        return jnp.concatenate([tile_of(tr, tc_own), tile_of(tr, other)], axis=1)

    def col_of(zi, xi, sign):
        zz = (z + sign * offset_of(zi) + NZ) % NZ
        xx = (x + sign * offset_of(xi) + NX) % NX
        return (zz * NX + xx) * 2 + k

    def over_group(a, b, fn):
        (z0, z1), (x0, x1) = GZ[a], GX[b]
        n = (z1 - z0) * (x1 - x0)
        width = x1 - x0
        if n == 1:
            fn(z0, x0)
        else:
            def step(i, carry):
                fn(z0 + i // width, x0 + i % width)
                return carry
            lax.fori_loop(0, n, step, 0)

    def forward_chunk(zi, xi):
        tc = col_of(zi, xi, -1)
        lhs = jnp.concatenate([tile_pair((y + j) % NY, tc) for j in range(NY)], axis=0)
        rhs = gathered[zi, xi].reshape(2 * node_rows, feat)
        acc[...] += jnp.dot(lhs, rhs, preferred_element_type=F32)

    def ag_compute(a, b):
        zs, xs = span(GZ[a]), span(GX[b])
        arrived(("ags", a, b), gathered.at[zs, xs, 1])
        over_group(a, b, forward_chunk)

    ag_pass(0, 0)

    key = jnp.where(
        lax.broadcasted_iota(jnp.int32, (1, slots), 1) < count[...],
        rows[0] * (NZ * NX * 2) + cols[0], -1,
    )
    best = [jnp.full((1, 128), slots, jnp.int32) for _ in range(2)]
    for k0 in range(0, slots, 128):
        n = min(128, slots - k0)
        part = key[:, k0:k0 + n]
        if n < 128:
            part = jnp.concatenate([part, jnp.full((1, 128 - n), -1, jnp.int32)], axis=1)
        column = jnp.broadcast_to(part, (128, 128)).T
        slot = lax.broadcasted_iota(jnp.int32, (128, 128), 0) + k0
        for h in range(2):
            place = lax.broadcasted_iota(jnp.int32, (128, 128), 1) + h * 128
            hit = jnp.where(column == place, slot, slots)
            best[h] = jnp.minimum(best[h], jnp.min(hit, axis=0, keepdims=True))
    inverse_v[...] = jnp.concatenate(best + [jnp.full((6, 128), slots, jnp.int32)], axis=0)
    to_smem = pltpu.make_async_copy(inverse_v, inverse, local_sem.at[1])
    to_smem.start()
    values[slots] = jnp.zeros((tile, tile), BF16)
    acc[...] = jnp.zeros_like(acc)
    to_smem.wait()
    tiles_in.wait()

    for n in range(1, len(DIAGS)):
        for a, b in DIAGS[n]:
            ag_pass(a, b)
        for a, b in DIAGS[n - 1]:
            ag_compute(a, b)
    for a, b in DIAGS[-1]:
        ag_compute(a, b)

    for j in (2, 1, 3):
        ysend[j] = acc[pl.ds(j * node_rows, node_rows)].astype(BF16)
        send(("y", j), ysend.at[j], yrecv.at[j], y_off(j))
    agg = acc[pl.ds(0, node_rows)]
    for j in (1, 3, 2):
        arrived(("y", j), yrecv.at[j])
        agg = agg + yrecv[j].astype(F32)
    agg_hi = agg.astype(BF16)
    agg_lo = (agg - agg_hi.astype(F32)).astype(BF16)
    pre = (
        jnp.dot(agg_hi, weight[...], preferred_element_type=F32)
        + jnp.dot(agg_lo, weight[...], preferred_element_type=F32)
        + bias[...]
    )
    sig = jax.nn.sigmoid(pre)
    dpre = (cotangent[...].astype(F32) * sig * (1.0 + pre * (1.0 - sig))).astype(BF16)
    dt[0] = dpre.astype(F32).T.astype(BF16)
    for j in (2, 1, 3):
        send(("d", j), dt.at[0], dt.at[j], y_off(j))
    act_out[...] = (pre * sig).astype(BF16)

    half = feat // 2
    aggt_hi = agg_hi.astype(F32).T.astype(BF16)
    aggt_lo = agg_lo.astype(F32).T.astype(BF16)
    bias_row = jnp.sum(dpre.astype(F32), axis=0, keepdims=True)
    bias_rows = jnp.concatenate([bias_row, jnp.zeros((7, feat), F32)], axis=0)
    gw = jnp.dot(aggt_hi, dpre, preferred_element_type=F32) + jnp.dot(
        aggt_lo, dpre, preferred_element_type=F32
    )
    for h in range(2):
        g1s[h, pl.ds(0, half)] = gw[h * half:(h + 1) * half]
        g1s[h, pl.ds(half, 8)] = bias_rows
    send("g1", g1s.at[1 - k], g1r, sibling)

    yrows, xrows = half // NY, half // NY // NX

    def g_step(n):
        if n == 2:
            arrived("g1", g1r)
            total = g1s[k] + g1r[...]
            for c in range(NY):
                g2s[c, pl.ds(0, yrows)] = total[c * yrows:(c + 1) * yrows]
                g2s[c, pl.ds(yrows, 8)] = total[half:half + 8]
            for j in (2, 1, 3):
                send(("g2", j), g2s.at[(y + j) % NY], g2r.at[y], y_off(j))
            g2r[y] = g2s[y]
        elif n == 3:
            for j in (1, 3, 2):
                arrived(("g2", j), g2r.at[(y - j + NY) % NY])
            total = g2r[0] + g2r[1] + g2r[2] + g2r[3]
            for c in range(NX):
                g3s[c, pl.ds(0, xrows)] = total[c * xrows:(c + 1) * xrows]
                g3s[c, pl.ds(xrows, 8)] = total[yrows:yrows + 8]
            for j in (2, 1, 3):
                send(("g3", j), g3s.at[(x + j) % NX], g3r.at[x], x_off(j))
            g3r[x] = g3s[x]
        elif n == 4:
            for j in (1, 3, 2):
                arrived(("g3", j), g3r.at[(x - j + NX) % NX])
            g4r[z] = g3r[0] + g3r[1] + g3r[2] + g3r[3]
            for j in (4, 3, 5, 2, 6, 1, 7):
                send(("g4", j), g4r.at[z], g4r.at[z], z_off(j))
        elif n == 5:
            for j in (1, 7, 2, 6, 3, 5, 4):
                arrived(("g4", j), g4r.at[(z - j + NZ) % NZ])
            total = g4r[0]
            for j in range(1, NZ):
                total = total + g4r[j]
            total = total * scale
            gb_out[...] = total[xrows:xrows + 1]
            g5[x] = total[0:xrows]
            for j in (2, 1, 3):
                send(("g5", j), g5.at[x], g5.at[x], x_off(j))
        elif n == 6:
            for j in (1, 3, 2):
                arrived(("g5", j), g5.at[(x - j + NX) % NX])
            g6[y] = g5[...].reshape(yrows, feat)
            for j in (2, 1, 3):
                send(("g6", j), g6.at[y], g6.at[y], y_off(j))
        elif n == 7:
            for j in (1, 3, 2):
                arrived(("g6", j), g6.at[(y - j + NY) % NY])
            g7[k] = g6[...].reshape(half, feat)
            send("g7", g7.at[k], g7.at[k], sibling)
        elif n == 8:
            arrived("g7", g7.at[1 - k])
            gw_out[...] = g7[...].reshape(feat, feat)

    for j in (1, 3, 2):
        arrived(("d", j), dt.at[j])

    def backward_chunk(zi, xi):
        tc = col_of(zi, xi, 1)
        lhs = jnp.concatenate([dt[j] for j in range(NY)], axis=1)
        rhs = jnp.concatenate([tile_pair((y - j + NY) % NY, tc) for j in range(NY)], axis=0)
        both = jnp.dot(lhs, rhs, preferred_element_type=F32)
        own32[zi, xi] = both[:, :tile]
        sibsend[zi, xi] = both[:, tile:].astype(BF16)

    def rs_compute(a, b):
        over_group(a, b, backward_chunk)
        zs, xs = span(GZ[a]), span(GX[b])
        send(("rss", a, b), sibsend.at[zs, xs], sibrecv.at[zs, xs], sibling)

    fpart1, fpart2 = (0, cut_feat), (cut_feat, feat)
    fwhole = (0, feat)

    def rs_z(a, b):
        f = span(fwhole if b == 0 else fpart2)
        xs = span(GX[b])
        s = GZ[a][0]
        moves = ((s, z_far),) if a == 4 else ((s, z_off(1)), (s + 1, z_off(-1)))
        for n, (src, dev) in enumerate(moves):
            send(("rsz", a, b, n), own.at[src, xs, f], from_z.at[src, xs, f], dev)

    def rs_z_arrived(a, b):
        f = span(fwhole if b == 0 else fpart2)
        for n, s in enumerate(range(*GZ[a])):
            arrived(("rsz", a, b, n), from_z.at[s, span(GX[b]), f])

    def rs_x(a, b):
        f = span(fwhole if a == 0 else fpart1)
        zs = span(GZ[a])
        s = GX[b][0]
        moves = ((s, x_far),) if b == 2 else ((s, x_off(1)), (s + 1, x_off(-1)))
        for n, (src, dev) in enumerate(moves):
            send(("rsx", a, b, n), own.at[zs, src, f], from_x.at[zs, src, f], dev)

    def rs_x_arrived(a, b):
        f = span(fwhole if a == 0 else fpart1)
        for n, s in enumerate(range(*GX[b])):
            arrived(("rsx", a, b, n), from_x.at[span(GZ[a]), s, f])

    def rs_sum(a, b, zi, xi, part):
        f = span(part)
        total = own32[zi, xi, f] + sibrecv[zi, xi, f].astype(F32)
        if b == 0 or part == fpart2:
            if a == 3:
                total = total + jnp.where(zi == 5 + k, from_z[7, xi, f].astype(F32), 0.0)
            elif a in (1, 2):
                total = total + from_z[zi + 2, xi, f].astype(F32)
            elif a == 0:
                total = total + from_z[1, xi, f].astype(F32) + from_z[2, xi, f].astype(F32)
        if a == 0 or part == fpart1:
            if b == 1:
                total = total + jnp.where(xi == 1 + k, from_x[zi, 3, f].astype(F32), 0.0)
            elif b == 0:
                total = total + from_x[zi, 1, f].astype(F32) + from_x[zi, 2, f].astype(F32)
        return total

    def rs_pass(a, b):
        zs, xs = span(GZ[a]), span(GX[b])
        arrived(("rss", a, b), sibrecv.at[zs, xs])
        if a < 4:
            rs_z_arrived(a + 1, b)
        if b < 2:
            rs_x_arrived(a, b + 1)
        if (a, b) == (0, 0):
            return

        def one(zi, xi):
            for part in (fpart1, fpart2):
                own[zi, xi, span(part)] = rs_sum(a, b, zi, xi, part).astype(BF16)

        over_group(a, b, one)
        if a > 0:
            rs_z(a, b)
        if b > 0:
            rs_x(a, b)

    order = DIAGS[::-1]
    for n in range(len(order) + 1):
        if n < len(order):
            for a, b in order[n]:
                rs_compute(a, b)
        if n >= 1:
            for a, b in order[n - 1]:
                rs_pass(a, b)
            g_step(n + 1)

    back_t = jnp.concatenate([rs_sum(0, 0, 0, 0, p) for p in (fpart1, fpart2)], axis=0)
    gf_out[...] = lax.dot_general(
        back_t.T.astype(BF16), weight[...], (((1,), (1,)), ((), ())), preferred_element_type=F32
    ).astype(BF16)
    for c in started:
        c.wait_send()


COPIES = 160


def on_device(features, weight, bias, cotangent, tile_values, tile_rows, tile_cols, tile_count):
    node_rows, feat = features.shape
    slots, tile = tile_values.shape[2], tile_values.shape[-1]
    half = feat // 2
    yrows, xrows = half // NY, half // NY // NX
    blocks = NZ * NX * 2
    scale = float((node_rows * blocks * NY) ** -0.5)
    vmem = pl.BlockSpec(memory_space=pltpu.VMEM)
    act, gf, gw, gb = pl.pallas_call(
        functools.partial(body, tile, slots, 80, 160, scale),
        out_shape=(
            jax.ShapeDtypeStruct((node_rows, feat), BF16),
            jax.ShapeDtypeStruct((node_rows, feat), BF16),
            jax.ShapeDtypeStruct((feat, feat), F32),
            jax.ShapeDtypeStruct((1, feat), F32),
        ),
        in_specs=[vmem] * 4 + [pl.BlockSpec(memory_space=pl.ANY)] + [vmem] * 3,
        out_specs=(vmem,) * 4,
        scratch_shapes=[
            pltpu.VMEM((slots + 1, tile, tile), BF16),
            pltpu.VMEM((8, 128), jnp.int32),
            pltpu.SMEM((8, 128), jnp.int32),
            pltpu.VMEM((NZ, NX, 2, node_rows, feat), BF16),
            pltpu.VMEM((NY * node_rows, feat), F32),
            pltpu.VMEM((NY, node_rows, feat), BF16),
            pltpu.VMEM((NY, node_rows, feat), BF16),
            pltpu.VMEM((NY, feat, node_rows), BF16),
            pltpu.VMEM((NZ, NX, feat, tile), F32),
            pltpu.VMEM((NZ, NX, feat, tile), BF16),
            pltpu.VMEM((NZ, NX, feat, tile), BF16),
            pltpu.VMEM((NZ, NX, feat, tile), BF16),
            pltpu.VMEM((NZ, NX, feat, tile), BF16),
            pltpu.VMEM((NZ, NX, feat, tile), BF16),
            pltpu.VMEM((2, half + 8, feat), F32),
            pltpu.VMEM((half + 8, feat), F32),
            pltpu.VMEM((NY, yrows + 8, feat), F32),
            pltpu.VMEM((NY, yrows + 8, feat), F32),
            pltpu.VMEM((NX, xrows + 8, feat), F32),
            pltpu.VMEM((NX, xrows + 8, feat), F32),
            pltpu.VMEM((NZ, xrows + 8, feat), F32),
            pltpu.VMEM((NX, xrows, feat), F32),
            pltpu.VMEM((NY, yrows, feat), F32),
            pltpu.VMEM((2, half, feat), F32),
            pltpu.SemaphoreType.DMA((COPIES,)),
            pltpu.SemaphoreType.DMA((COPIES,)),
            pltpu.SemaphoreType.DMA((2,)),
        ],
        compiler_params=pltpu.CompilerParams(
            collective_id=0, has_side_effects=True, vmem_limit_bytes=48 * 1024 * 1024
        ),
        cost_estimate=pl.CostEstimate(
            flops=4 * NY * node_rows * blocks * node_rows * feat,
            bytes_accessed=slots * tile * tile * 2,
            transcendentals=node_rows * feat,
        ),
    )(features, weight, bias.reshape(1, feat), cotangent, tile_values, tile_rows, tile_cols, tile_count)
    return act, gf, gw, gb.reshape(feat)


def solution(mesh):
    in_specs = (
        P(("row", "rep"), None),
        P(),
        P(),
        P(("row", "rep"), None),
        P("row", "rep", None, None, None),
        P("row", "rep", None),
        P("row", "rep", None),
        P("row", "rep"),
    )
    out_specs = (P(("row", "rep"), None), P(("row", "rep"), None), P(), P())
    return jax.shard_map(
        on_device, mesh=mesh, in_specs=in_specs, out_specs=out_specs, check_vma=False
    )
```

time: 720 us -> 84.3 us (0.12)
  waiting for transfers between devices: 427 us -> 0 us
  blocking collectives: 89.9 us -> 0 us
  Pallas kernels: 0 us -> 75.5 us
  local copies, waits for them, and re-layouts: 74.8 us -> 7.14 us
  other arithmetic: 61.5 us -> 0 us
  matrix products: 50.3 us -> 0 us
  between operations: 14.5 us -> 1.3 us
    psum x1 -> x0, waiting for transfers between devices: 255 us -> none  [on_device(): lax.psum((weight_term, bias_term), ('row', 'rep'))]
    reduce_scatter x2 -> x0, waiting for transfers between devices: 88.9 us -> none  [the longest x1 69.6 us: on_device(): back = lax.psum_scatter(terms, 'row', scatter_dimension=0, tiled=True)]
    all_gather x1 -> x0, waiting for transfers between devices: 83.4 us -> none  [on_device(): gathered = lax.all_gather(xw, 'row', axis=0, tiled=True)]
    psum x1 -> x0, blocking collectives: 80 us -> none  [on_device(): lax.psum((weight_term, bias_term), ('row', 'rep'))]
    pallas_call x0 -> x1, Pallas kernels: none -> 75.5 us  [on_device(): pl.pallas_call(functools.partial(body, tile, slots, 80, 160, scale), out_...]
    scatter-add x1 -> x0, other arithmetic: 57.6 us -> none  [on_device(): jax.ops.segment_sum(back_prod, cols, num_segments=tcols)]
    dot_general x6 -> x0, matrix products: 50.3 us -> none  [the longest x1 15.8 us: on_device(): jnp.einsum('kab,kaf->kbf', values, dtaken, preferred_element_type=jnp.flo...]
    dot_general x2 -> x0, local copies, waits for them, and re-layouts: 25.7 us -> none  [the longest x1 24.8 us: on_device(): jnp.einsum('kab,kbf->kaf', values, taken, preferred_element_type=jnp.floa...]
  transfers between devices with their start and end apart: 4 -> 0, of which waited for: 4 -> 0; matrix products, arithmetic and copies ran while one was open for 0% -> 0% of each run, Pallas kernels for 0% -> 0%
where the time goes in v1:
time: 84.3 us; the launch traced here: 83.9 us
  Pallas kernels  75.5 us (90%)
  local copies, waits for them, and re-layouts  7.14 us (8%)
  between operations  1.3 us (2%)
    pallas_call x1, Pallas kernels, on_device(): pl.pallas_call(functools.partial(body, tile, slots, 80, 160, scale), out_...  75.5 us
    unnamed x16, local copies, waits for them, and re-layouts  7.14 us

profile of v1, /device:TPU:1, one launch (start us, length us, event | category | flops | bytes accessed | tf_op | source)
XLA Modules:
  0.0 83.9 jit_solution(1491393253804631448)
XLA Ops:
  1.3 0.0 copy-start
  1.3 0.9 %copy-done = bf16[256,256]{1,0:T(8,128)(2,1)S(1)} copy-done((bf16[256,256]{1,0:T(8,128)(2,1)S(1)}, bf16[256,256]{1,0:T(8,128)(2,1)}, u32[]{:S(2)}) %copy-start) | copy-done | bytes 131096
  2.2 0.0 copy-start.1
  2.2 0.8 copy-done.1
  3.0 0.0 copy-start.2
  3.0 0.8 copy-done.2
  3.9 0.0 copy-start.3
  3.9 0.7 copy-done.3
  4.5 0.0 copy-start.4
  4.5 0.7 copy-done.4
  5.2 0.0 copy-start.5
  5.2 0.7 copy-done.5
  5.9 75.5 %shard_map.111 = (bf16[128,256]{1,0:T(8,128)(2,1)S(1)}, bf16[128,256]{1,0:T(8,128)(2,1)S(1)}, f32[256,256]{1,0:T(8,128)S(1)}, f32[1,256]{1,0:T(1,128)S(1)}) custom-call(bf16[128,256]{1,0:T(8,128)(2,1)S(1)} %copy-done.1, bf16[256,256]{1,0:T(8,128)(2,1)S(1)} %copy-done, f32[1,256]{1,0:T(1,128)S(1)} %bitcast.3, bf16[128,256]{1,0:T(8,128)(2,1)S(1)} %copy-done.2, ...), custom_call_target="tpu_custom_call" | custom-call | flops 4294967296 | bytes 6291456 | tf_op jit(solution)/shard_map/pallas_call | solution.py:410
  81.4 0.6 copy.17
  82.0 0.6 copy.18
  82.7 0.7 copy.19
  83.4 0.6 copy.20
Async XLA Ops:
  1.3 0.9 %copy-start = (bf16[256,256]{1,0:T(8,128)(2,1)S(1)}, bf16[256,256]{1,0:T(8,128)(2,1)}, u32[]{:S(2)}) copy-start(bf16[256,256]{1,0:T(8,128)(2,1)} %weight.1) | copy-start | bytes 393220
  2.2 0.8 %copy-start.1 = (bf16[128,256]{1,0:T(8,128)(2,1)S(1)}, bf16[128,256]{1,0:T(8,128)(2,1)}, u32[]{:S(2)}) copy-start(bf16[128,256]{1,0:T(8,128)(2,1)} %features.1) | copy-start | bytes 196612
  3.0 0.8 %copy-start.2 = (bf16[128,256]{1,0:T(8,128)(2,1)S(1)}, bf16[128,256]{1,0:T(8,128)(2,1)}, u32[]{:S(2)}) copy-start(bf16[128,256]{1,0:T(8,128)(2,1)} %cotangent.1) | copy-start | bytes 196612
  3.9 0.7 copy-start.3
  4.5 0.7 copy-start.4
  5.2 0.7 copy-start.5

commit v2 on v0

v2 whole, which is shorter than its diff:
```python
import functools

import jax
import jax.numpy as jnp
from jax import lax
from jax.experimental import pallas as pl
from jax.experimental.pallas import tpu as pltpu
from jax.sharding import PartitionSpec as P

MESH = pl.DeviceIdType.MESH
F32 = jnp.float32
BF16 = jnp.bfloat16
NZ, NX, NY = 8, 4, 4
Z_COLUMN = ({0: ((3, 2), (4, -2), (1, 1), (2, -1)), 3: ((5, 1),), 4: ((6, -1),)}, (3, 4), 7, 2)
X_ROW = ({0: ((3, 2), (1, 1), (2, -1))}, (), 0, 0)
X_FIRST = ({0: ((1, 1), (2, -1))}, (1, 2), 3, 1)
Z_SECOND = ({0: ((3, 2), (4, -2), (1, 1), (2, -1)), 3: ((5, 1),), 4: ((6, -1),)}, (3, 4), 7, 2)
Z_REACH, X_REACH = ((1, 2), (1, 2))
PARTS = ((1, 0, 96), (2, 96, 128))
AG_ORDER = (
    (0,0,0,0), (0,0,0,1), (1,0,0), (0,0,3,0), (0,3,0,0), (0,4,0,0), (0,0,1,0), (0,0,2,0), (0,1,0,0), (0,0,3,1),
    (0,2,0,0), (1,0,3), (0,0,2,1), (0,0,1,1), (1,0,2), (1,0,1), (0,3,0,1), (0,4,0,1), (1,3,0), (1,4,0), (0,1,0,1),
    (0,2,0,1), (1,1,0), (1,2,0), (0,3,1,0), (0,3,2,0), (2,(0,0),(0,3),(0,2),(0,1)), (0,5,0,0), (0,4,1,0), (0,4,2,0),
    (2,(3,0),(4,0),(1,0),(2,0)), (0,7,0,0), (0,1,1,0), (0,1,2,0), (0,3,3,1), (0,6,0,0), (0,1,3,1), (0,2,1,0),
    (0,2,2,0), (0,3,3,0), (1,3,3), (0,4,3,1), (0,3,2,1), (0,2,3,1), (1,3,2), (0,1,2,1), (1,1,2), (0,5,1,0), (0,5,2,0),
    (0,4,2,1), (1,4,2), (0,4,3,0), (1,4,3), (0,3,1,1), (0,2,2,1), (1,3,1), (1,2,2), (0,1,1,1), (1,1,1), (0,5,0,1),
    (1,5,0), (0,7,1,0), (0,7,2,0), (2,(3,3),(3,2),(1,2),(4,2)), (0,4,1,1), (1,4,1), (0,1,3,0), (0,2,1,1), (1,1,3),
    (1,2,1), (2,(4,3),(3,1),(2,2),(1,1)), (0,7,0,1), (1,7,0), (0,6,1,0), (0,6,2,0), (0,5,3,1), (0,6,0,1), (1,6,0),
    (0,2,3,0), (1,2,3), (0,7,3,1), (2,(5,0),(4,1),(1,3),(2,1)), (0,5,3,0), (1,5,3), (0,5,2,1), (0,6,3,1), (1,5,2),
    (0,7,3,0), (1,7,3), (0,7,2,1), (1,7,2), (2,(7,0),(6,0),(2,3),(5,3)), (0,6,3,0), (0,5,1,1), (0,6,2,1), (1,6,3),
    (1,5,1), (1,6,2), (0,7,1,1), (1,7,1), (0,6,1,1), (1,6,1), (2,(5,2),(7,3),(7,2),(6,3)), (2,(5,1),(6,2)),
    (2,(7,1),(6,1)),
)
RS_ORDER = (
    (2,(7,3),(5,3),(6,3),(7,1)), (2,(7,2),(5,1),(6,1),(6,2)), (2,(5,2),(4,3),(3,3),(1,3)), (0,7,3,0), (0,7,3,1),
    (0,5,3,0), (0,5,3,1), (0,6,3,0), (0,6,3,1), (2,(2,3),(7,0),(5,0),(6,0)), (0,7,1,1), (0,7,2,1), (0,5,1,1),
    (2,(3,1),(4,1),(4,2),(3,2)), (0,6,1,1), (0,6,2,1), (0,5,2,1), (2,(2,1),(1,1),(2,2),(1,2)), (0,4,3,0), (0,3,3,0),
    (0,1,3,0), (0,7,1,0), (0,7,2,0), (0,2,3,0), (0,7,0,1), (0,1,3,1), (0,5,1,0), (0,5,2,0), (0,3,3,1), (0,4,3,1),
    (0,2,3,1), (0,6,1,0), (0,6,2,0), (0,5,0,1), (0,6,0,1), (2,(4,0),(3,0),(0,3),(1,0)), (0,2,1,1), (0,4,1,0),
    (0,4,2,0), (0,1,1,1), (2,(2,0),(0,1),(0,2),(0,0)), (0,2,2,1), (0,3,1,0), (0,3,2,0), (0,1,2,1), (0,3,1,1),
    (0,4,1,1), (0,1,1,0), (0,4,2,1), (0,3,2,1), (0,1,2,0), (0,0,3,0), (0,1,0,1), (0,2,0,1), (0,7,0,0), (0,0,1,0),
    (0,2,1,0), (0,2,2,0), (0,0,2,0), (0,0,3,1), (0,5,0,0), (0,4,0,1), (0,3,0,1), (0,6,0,0), (0,0,1,1), (0,0,2,1),
    (0,1,0,0), (0,3,0,0), (0,4,0,0), (0,2,0,0), (0,0,0,1), (0,0,0,0),
)
G_AT = (34, 64, 69, 71)


def moves(kind, zi, xi):
    if kind == 1:
        if xi == 0:
            yield "z", zi, Z_COLUMN
        yield "x", xi, (X_FIRST if zi else X_ROW)
    else:
        if zi == 0:
            yield "x", xi, X_ROW
        yield "z", zi, (Z_SECOND if xi else Z_COLUMN)


def children(kind, zi, xi):
    found = []
    for axis, at, (steps, pair, last, hops) in moves(kind, zi, xi):
        for to, h in steps.get(at, ()):
            found.append((axis, (to, xi) if axis == "z" else (zi, to), h, None))
        if at in pair:
            found.append((axis, (last, xi) if axis == "z" else (zi, last), hops, pair.index(at)))
    return found


def body(
    tile, slots, scale,
    features_hbm, weight_hbm, bias_hbm, cotangent_hbm, values_hbm, rows_hbm, cols_hbm, count_hbm,
    act_out, gf_out, gw_out, gb_out,
    features, weight, bias, cotangent, rows, cols, count,
    values, inverse_v, inverse, gathered, acc, ysend, yrecv, dt,
    own32, own, sibsend, sibrecv, landed, back_t,
    g1s, g1r, g2s, g2r, g4r, g5, g7,
    send_sem, recv_sem, local_sem,
):
    r = lax.axis_index("row")
    y = lax.axis_index("rep")
    z = r // (2 * NX)
    x = (r // 2) % NX
    k = r % 2
    node_rows, feat = features_hbm.shape
    half = feat // 2

    def at(zz, xx, kk, yy):
        return ((zz * NX + xx) * 2 + kk, yy)

    def z_off(d):
        return at((z + d + NZ) % NZ, x, k, y)

    def x_off(d):
        return at(z, (x + d + NX) % NX, k, y)

    def y_off(d):
        return at(z, x, k, (y + d + NY) % NY)

    def toward(axis, hops, pair):
        d = hops if pair is None else hops * (1 - 2 * k)
        return z_off(d) if axis == "z" else x_off(d)

    sibling = at(z, x, 1 - k, y)
    names = {}
    groups = {}

    def copy(name, group, src, dst, device):
        i = names.setdefault(name, len(names))
        j = groups.setdefault(group, len(groups))
        return pltpu.make_async_remote_copy(
            src_ref=src, dst_ref=dst, send_sem=send_sem.at[j], recv_sem=recv_sem.at[i],
            device_id=device, device_id_type=MESH,
        )

    def send(name, group, src, dst, device):
        copy(name, group, src, dst, device).start()

    def arrived(name, dst):
        copy(name, "ag", dst, dst, sibling).wait_recv()

    def sent(group, src):
        copy("y", group, src, src, sibling).wait_send()

    loads = [
        pltpu.make_async_copy(src, dst, local_sem.at[n])
        for n, (src, dst) in enumerate((
            (features_hbm, features), (rows_hbm, rows), (cols_hbm, cols), (count_hbm, count),
            (weight_hbm, weight), (bias_hbm, bias), (cotangent_hbm, cotangent),
            (values_hbm.at[0, 0], values.at[pl.ds(0, slots)]),
        ))
    ]
    for load in loads:
        load.start()
    barrier = pltpu.get_barrier_semaphore()
    peers = (
        [z_off(s * d) for d in Z_REACH for s in (1, -1)]
        + [x_off(s * d) for d in X_REACH for s in (1, -1)]
        + [y_off(d) for d in range(1, NY)]
        + [sibling]
    )
    for p in peers:
        pl.semaphore_signal(barrier, inc=1, device_id=p, device_id_type=MESH)
    loads[0].wait()
    pl.semaphore_wait(barrier, len(peers))

    seen = set()

    def ag_piece(zi, xi, p):
        kind, r0, r1 = PARTS[p]
        part = pl.ds(r0, r1 - r0)
        if (zi, xi) == (0, 0):
            source = features.at[part]
        else:
            source = gathered.at[zi, xi, 0, part]
            arrived(("ag", zi, xi, p), source)
        for axis, (zd, xd), hops, pair in children(kind, zi, xi):
            origin = source
            if pair is not None:
                if (zd, xd, p) not in seen:
                    seen.add((zd, xd, p))
                    continue
                if axis == "z":
                    origin = gathered.at[zi - pair + k, xi, 0, part]
                else:
                    origin = gathered.at[zi, xi - pair + k, 0, part]
            send(("ag", zd, xd, p), "ag", origin, gathered.at[zd, xd, 0, part], toward(axis, hops, pair))

    batch_of = {c: n for n, (what, *where) in enumerate(AG_ORDER) if what == 2 for c in where}

    def ag_share(zi, xi):
        source = features if (zi, xi) == (0, 0) else gathered.at[zi, xi, 0]
        send(("share", batch_of[zi, xi]), "ag", source, gathered.at[zi, xi, 1], sibling)

    def offset_of(slot):
        return (slot + 1) // 2 * (2 * (slot % 2) - 1)

    def tile_of(tr, tc):
        p = tr * (NZ * NX * 2) + tc
        return values[inverse[p // 128, p % 128]]

    def tile_pair(tr, tc_own):
        return jnp.concatenate([tile_of(tr, tc_own), tile_of(tr, tc_own + 1 - 2 * k)], axis=1)

    def col_of(zi, xi, sign):
        zz = (z + sign * offset_of(zi) + NZ) % NZ
        xx = (x + sign * offset_of(xi) + NX) % NX
        return (zz * NX + xx) * 2 + k

    def forward(chunks):
        arrived(("share", batch_of[chunks[0]]), gathered.at[pl.ds(0, len(chunks)), 0, 1])
        lhs = jnp.concatenate([
            jnp.concatenate([tile_pair((y + j) % NY, col_of(zi, xi, -1)) for zi, xi in chunks], axis=1)
            for j in range(NY)
        ], axis=0)
        rhs = jnp.concatenate([gathered[zi, xi].reshape(2 * node_rows, feat) for zi, xi in chunks], axis=0)
        term = jnp.dot(lhs, rhs, preferred_element_type=F32)
        if (0, 0) in chunks:
            acc[...] = term
        else:
            acc[...] += term

    todo = list(AG_ORDER)
    while todo[0][:3] == (0, 0, 0):
        ag_piece(*todo.pop(0)[1:])
    gathered[0, 0, 0] = features[...]

    for load in loads[1:4]:
        load.wait()
    key = jnp.where(
        lax.broadcasted_iota(jnp.int32, (1, slots), 1) < count[...],
        rows[0] * (NZ * NX * 2) + cols[0], -1,
    )
    best = [jnp.full((1, 128), slots, jnp.int32) for _ in range(2)]
    for k0 in range(0, slots, 128):
        n = min(128, slots - k0)
        part = key[:, k0:k0 + n]
        if n < 128:
            part = jnp.concatenate([part, jnp.full((1, 128 - n), -1, jnp.int32)], axis=1)
        column = jnp.broadcast_to(part, (128, 128)).T
        slot = lax.broadcasted_iota(jnp.int32, (128, 128), 0) + k0
        for h in range(2):
            place = lax.broadcasted_iota(jnp.int32, (128, 128), 1) + h * 128
            hit = jnp.where(column == place, slot, slots)
            best[h] = jnp.minimum(best[h], jnp.min(hit, axis=0, keepdims=True))
    inverse_v[...] = jnp.concatenate(best + [jnp.full((6, 128), slots, jnp.int32)], axis=0)
    to_smem = pltpu.make_async_copy(inverse_v, inverse, local_sem.at[len(loads)])
    to_smem.start()
    values[slots] = jnp.zeros((tile, tile), BF16)

    ready = False
    for what, *where in todo:
        if what == 0:
            ag_piece(*where)
        elif what == 1:
            ag_share(*where)
        else:
            if not ready:
                to_smem.wait()
                for load in loads[4:]:
                    load.wait()
                ready = True
            forward(where)

    for j in (2, 1, 3):
        ysend[j] = acc[pl.ds(j * node_rows, node_rows)].astype(BF16)
        send("y", "yd", ysend.at[j], yrecv.at[j], y_off(j))
    agg = acc[pl.ds(0, node_rows)]
    arrived("y", yrecv.at[pl.ds(1, 3)])
    for j in (1, 3, 2):
        agg = agg + yrecv[j].astype(F32)
    agg_hi = agg.astype(BF16)
    agg_lo = (agg - agg_hi.astype(F32)).astype(BF16)
    halves = []
    for h in range(2):
        f = pl.ds(h * half, half)
        pre = (
            jnp.dot(agg_hi, weight[:, f], preferred_element_type=F32)
            + jnp.dot(agg_lo, weight[:, f], preferred_element_type=F32)
            + bias[:, f]
        )
        sig = jax.nn.sigmoid(pre)
        dpre = (cotangent[:, f].astype(F32) * sig * (1.0 + pre * (1.0 - sig))).astype(BF16)
        dt[0, f] = dpre.astype(F32).T.astype(BF16)
        for j in (2, 1, 3):
            send(("d", h), "yd", dt.at[0, f], dt.at[j, f], y_off(j))
        act_out[:, f] = (pre * sig).astype(BF16)
        halves.append(dpre)
    dpre = jnp.concatenate(halves, axis=1)

    aggt_hi = agg_hi.astype(F32).T.astype(BF16)
    aggt_lo = agg_lo.astype(F32).T.astype(BF16)
    bias_row = jnp.sum(dpre.astype(F32), axis=0, keepdims=True)
    bias_rows = jnp.concatenate([bias_row, jnp.zeros((7, feat), F32)], axis=0)
    gw = jnp.dot(aggt_hi, dpre, preferred_element_type=F32) + jnp.dot(
        aggt_lo, dpre, preferred_element_type=F32
    )
    for h in range(2):
        g1s[h, pl.ds(0, half)] = gw[h * half:(h + 1) * half]
        g1s[h, pl.ds(half, 8)] = bias_rows
    send("g1", "g1", g1s.at[1 - k], g1r, sibling)

    q = y * NX + x
    square = [(dy, dx) for dy in (2, 1, 3, 0) for dx in (2, 1, 3, 0) if (dy, dx) != (0, 0)]

    def in_square(dy, dx):
        yy, xx = (y + dy) % NY, (x + dx) % NX
        return yy * NX + xx, at(z, xx, k, yy)

    def g_step(n):
        if n == 0:
            arrived("g1", g1r)
            total = g1s[k] + g1r[...]
            for c in range(NY * NX):
                g2s[c, pl.ds(0, 8)] = total[c * 8:(c + 1) * 8]
                g2s[c, pl.ds(8, 8)] = total[half:half + 8]
            for dy, dx in square:
                c, device = in_square(dy, dx)
                send("g2", "g2", g2s.at[c], g2r.at[q], device)
            g2r[q] = g2s[q]
        elif n == 1:
            arrived("g2", g2r.at[pl.ds(0, NY * NX - 1)])
            total = g2r[0]
            for c in range(1, NY * NX):
                total = total + g2r[c]
            g4r[z] = total
            for j in (4, 3, 5, 2, 6, 1, 7):
                send("g4", "g4", g4r.at[z], g4r.at[z], z_off(j))
        elif n == 2:
            arrived("g4", g4r.at[pl.ds(0, NZ - 1)])
            total = g4r[0]
            for j in range(1, NZ):
                total = total + g4r[j]
            total = total * scale
            gb_out[...] = total[8:9]
            g5[q] = total[0:8]
            for dy, dx in square:
                send("g5", "g5", g5.at[q], g5.at[q], in_square(dy, dx)[1])
        elif n == 3:
            arrived("g5", g5.at[pl.ds(0, NY * NX - 1)])
            g7[k] = g5[...].reshape(half, feat)
            send("g7", "g7", g7.at[k], g7.at[k], sibling)
        elif n == 4:
            arrived("g7", g7.at[1 - k])
            gw_out[...] = g7[...].reshape(feat, feat)

    g_step(0)
    sent("ag", values.at[pl.ds(0, 2 * (2 * NZ * NX - 1))])

    for h in range(2):
        arrived(("d", h), dt.at[pl.ds(1, NY - 1), pl.ds(h * half, half)])

    back_batch = {c: n for n, (what, *where) in enumerate(RS_ORDER) if what == 2 for c in where}
    back_size = {n: len(where) for n, (what, *where) in enumerate(RS_ORDER) if what == 2}

    def backward(chunks):
        lhs = jnp.concatenate([dt[j] for j in range(NY)], axis=1)
        for zi, xi in chunks:
            tc = col_of(zi, xi, 1)
            rhs = jnp.concatenate([tile_pair((y - j + NY) % NY, tc) for j in range(NY)], axis=0)
            both = jnp.dot(lhs, rhs, preferred_element_type=F32)
            own32[zi, xi] = both[:, :tile]
            sibsend[zi, xi] = both[:, tile:].astype(BF16)
        for zi, xi in chunks:
            send(("rss", back_batch[zi, xi]), "rs", sibsend.at[zi, xi], sibrecv.at[zi, xi], sibling)

    parent = {}
    for p, (kind, _, _) in enumerate(PARTS):
        for zi in range(NZ):
            for xi in range(NX):
                for axis, (zd, xd), hops, pair in children(kind, zi, xi):
                    parent[zd, xd, p] = (axis, hops, pair)

    waited = set()

    def once(name, dst):
        if name not in waited:
            waited.add(name)
            arrived(name, dst)

    def rs_piece(zi, xi, p):
        kind, r0, r1 = PARTS[p]
        f = pl.ds(2 * r0, 2 * (r1 - r0))
        n = back_batch[zi, xi]
        once(("rss", n), sibrecv.at[pl.ds(0, back_size[n]), 0])
        below = children(kind, zi, xi)
        for _, (zd, xd), _, _ in below:
            once(("rs", zd, xd, p), landed.at[zd, xd, f])
        total = own32[zi, xi, f] + sibrecv[zi, xi, f].astype(F32)
        for _, (zd, xd), _, pair in below:
            term = landed[zd, xd, f].astype(F32)
            total = total + (term if pair is None else jnp.where(k == pair, term, 0.0))
        if (zi, xi) == (0, 0):
            back_t[f] = total
            return
        own[zi, xi, f] = total.astype(BF16)
        axis, hops, pair = parent[zi, xi, p]
        send(("rs", zi, xi, p), "rs", own.at[zi, xi, f], landed.at[zi, xi, f], toward(axis, hops, pair))

    steps = {at: n + 1 for n, at in enumerate(G_AT)}
    for i, (what, *where) in enumerate(RS_ORDER):
        if what == 0:
            rs_piece(*where)
        else:
            backward(where)
        if i in steps:
            g_step(steps[i])

    gf_out[...] = lax.dot_general(
        back_t[...].T.astype(BF16), weight[...], (((1,), (1,)), ((), ())), preferred_element_type=F32
    ).astype(BF16)
    sent("yd", values.at[pl.ds(0, 4 * (NY - 1))])
    sent("rs", values.at[pl.ds(0, 2 * (2 * NZ * NX - 1))])
    sent("g1", g1r)
    sent("g2", g2r.at[pl.ds(0, NY * NX - 1)])
    sent("g4", g4r.at[pl.ds(0, NZ - 1)])
    sent("g5", g5.at[pl.ds(0, NY * NX - 1)])
    sent("g7", g7.at[0])


COPIES = 149
GROUPS = 8


def on_device(features, weight, bias, cotangent, tile_values, tile_rows, tile_cols, tile_count):
    node_rows, feat = features.shape
    slots, tile = tile_values.shape[2], tile_values.shape[-1]
    half = feat // 2
    blocks = NZ * NX * 2
    scale = float((node_rows * blocks * NY) ** -0.5)
    vmem = pl.BlockSpec(memory_space=pltpu.VMEM)
    act, gf, gw, gb = pl.pallas_call(
        functools.partial(body, tile, slots, scale),
        out_shape=(
            jax.ShapeDtypeStruct((node_rows, feat), BF16),
            jax.ShapeDtypeStruct((node_rows, feat), BF16),
            jax.ShapeDtypeStruct((feat, feat), F32),
            jax.ShapeDtypeStruct((1, feat), F32),
        ),
        in_specs=[pl.BlockSpec(memory_space=pltpu.HBM)] * 8,
        out_specs=(vmem,) * 4,
        scratch_shapes=[
            pltpu.VMEM((node_rows, feat), BF16),
            pltpu.VMEM((feat, feat), BF16),
            pltpu.VMEM((1, feat), F32),
            pltpu.VMEM((node_rows, feat), BF16),
            pltpu.VMEM((1, 1, slots), jnp.int32),
            pltpu.VMEM((1, 1, slots), jnp.int32),
            pltpu.VMEM((1, 1), jnp.int32),
            pltpu.VMEM((slots + 1, tile, tile), BF16),
            pltpu.VMEM((8, 128), jnp.int32),
            pltpu.SMEM((8, 128), jnp.int32),
            pltpu.VMEM((NZ, NX, 2, node_rows, feat), BF16),
            pltpu.VMEM((NY * node_rows, feat), F32),
            pltpu.VMEM((NY, node_rows, feat), BF16),
            pltpu.VMEM((NY, node_rows, feat), BF16),
            pltpu.VMEM((NY, feat, node_rows), BF16),
            pltpu.VMEM((NZ, NX, feat, tile), F32),
            pltpu.VMEM((NZ, NX, feat, tile), BF16),
            pltpu.VMEM((NZ, NX, feat, tile), BF16),
            pltpu.VMEM((NZ, NX, feat, tile), BF16),
            pltpu.VMEM((NZ, NX, feat, tile), BF16),
            pltpu.VMEM((feat, tile), F32),
            pltpu.VMEM((2, half + 8, feat), F32),
            pltpu.VMEM((half + 8, feat), F32),
            pltpu.VMEM((NY * NX, 16, feat), F32),
            pltpu.VMEM((NY * NX, 16, feat), F32),
            pltpu.VMEM((NZ, 16, feat), F32),
            pltpu.VMEM((NY * NX, 8, feat), F32),
            pltpu.VMEM((2, half, feat), F32),
            pltpu.SemaphoreType.DMA((GROUPS,)),
            pltpu.SemaphoreType.DMA((COPIES,)),
            pltpu.SemaphoreType.DMA((9,)),
        ],
        compiler_params=pltpu.CompilerParams(
            collective_id=0, has_side_effects=True, vmem_limit_bytes=64 * 1024 * 1024
        ),
        cost_estimate=pl.CostEstimate(
            flops=4 * NY * node_rows * blocks * node_rows * feat,
            bytes_accessed=slots * tile * tile * 2,
            transcendentals=node_rows * feat,
        ),
    )(features, weight, bias.reshape(1, feat), cotangent, tile_values, tile_rows, tile_cols, tile_count)
    return act, gf, gw, gb.reshape(feat)


def solution(mesh):
    in_specs = (
        P(("row", "rep"), None),
        P(),
        P(),
        P(("row", "rep"), None),
        P("row", "rep", None, None, None),
        P("row", "rep", None),
        P("row", "rep", None),
        P("row", "rep"),
    )
    out_specs = (P(("row", "rep"), None), P(("row", "rep"), None), P(), P())
    return jax.shard_map(
        on_device, mesh=mesh, in_specs=in_specs, out_specs=out_specs, check_vma=False
    )
```

time: 720 us -> 76.3 us (0.11)
  waiting for transfers between devices: 427 us -> 0 us
  blocking collectives: 89.9 us -> 0 us
  Pallas kernels: 0 us -> 69 us
  local copies, waits for them, and re-layouts: 74.8 us -> 5.81 us
  other arithmetic: 61.5 us -> 0 us
  matrix products: 50.3 us -> 0 us
  between operations: 14.5 us -> 1.29 us
    psum x1 -> x0, waiting for transfers between devices: 255 us -> none  [on_device(): lax.psum((weight_term, bias_term), ('row', 'rep'))]
    reduce_scatter x2 -> x0, waiting for transfers between devices: 88.9 us -> none  [the longest x1 69.6 us: on_device(): back = lax.psum_scatter(terms, 'row', scatter_dimension=0, tiled=True)]
    all_gather x1 -> x0, waiting for transfers between devices: 83.4 us -> none  [on_device(): gathered = lax.all_gather(xw, 'row', axis=0, tiled=True)]
    psum x1 -> x0, blocking collectives: 80 us -> none  [on_device(): lax.psum((weight_term, bias_term), ('row', 'rep'))]
    pallas_call x0 -> x1, Pallas kernels: none -> 69 us  [on_device(): pl.pallas_call(functools.partial(body, tile, slots, scale), out_shape=(ja...]
    scatter-add x1 -> x0, other arithmetic: 57.6 us -> none  [on_device(): jax.ops.segment_sum(back_prod, cols, num_segments=tcols)]
    dot_general x6 -> x0, matrix products: 50.3 us -> none  [the longest x1 15.8 us: on_device(): jnp.einsum('kab,kaf->kbf', values, dtaken, preferred_element_type=jnp.flo...]
    dot_general x2 -> x0, local copies, waits for them, and re-layouts: 25.7 us -> none  [the longest x1 24.8 us: on_device(): jnp.einsum('kab,kbf->kaf', values, taken, preferred_element_type=jnp.floa...]
  transfers between devices with their start and end apart: 4 -> 0, of which waited for: 4 -> 0; matrix products, arithmetic and copies ran while one was open for 0% -> 0% of each run, Pallas kernels for 0% -> 0%
where the time goes in v2:
time: 76.3 us; the launch traced here: 76.1 us
  Pallas kernels  69 us (90%)
  local copies, waits for them, and re-layouts  5.81 us (8%)
  between operations  1.29 us (2%)
    pallas_call x1, Pallas kernels, on_device(): pl.pallas_call(functools.partial(body, tile, slots, scale), out_shape=(ja...  69 us
    unnamed x4, local copies, waits for them, and re-layouts  5.81 us

profile of v2, /device:TPU:1, one launch (start us, length us, event | category | flops | bytes accessed | tf_op | source)
XLA Modules:
  0.0 76.1 jit_solution(1760166341485289690)
XLA Ops:
  1.3 69.0 %shard_map.111 = (bf16[128,256]{1,0:T(8,128)(2,1)}, bf16[128,256]{1,0:T(8,128)(2,1)}, f32[256,256]{1,0:T(8,128)}, f32[1,256]{1,0:T(1,128)}) custom-call(bf16[128,256]{1,0:T(8,128)(2,1)} %features_hbm.1, bf16[256,256]{1,0:T(8,128)(2,1)} %weight_hbm.1, f32[1,256]{1,0:T(1,128)} %bitcast.3, bf16[128,256]{1,0:T(8,128)(2,1)} %cotangent_hbm.1, ...), custom_call_target="tpu_custom_call" | custom-call | flops 4294967296 | bytes 6291456 | tf_op jit(solution)/shard_map/pallas_call | solution.py:411
  70.3 1.5 %copy.17 = bf16[128,256]{1,0:T(8,128)(2,1)} copy(bf16[128,256]{1,0:T(8,128)(2,1)} %get-tuple-element.16) | data formatting | bytes 131072
  71.8 1.5 %copy.18 = bf16[128,256]{1,0:T(8,128)(2,1)} copy(bf16[128,256]{1,0:T(8,128)(2,1)} %get-tuple-element.17) | data formatting | bytes 131072
  73.3 1.7 %copy.19 = f32[256,256]{1,0:T(8,128)} copy(f32[256,256]{1,0:T(8,128)} %get-tuple-element.18) | data formatting | bytes 524288
  74.9 1.2 %copy.20 = f32[256]{0:T(256)} copy(f32[256]{0:T(256)} %bitcast.2) | data formatting | bytes 2048

commit v3 on v2

--- a/solution.py
+++ b/solution.py
@@ -11,54 +11,65 @@
 F32 = jnp.float32
 BF16 = jnp.bfloat16
 NZ, NX, NY = 8, 4, 4
-Z_COLUMN = ({0: ((3, 2), (4, -2), (1, 1), (2, -1)), 3: ((5, 1),), 4: ((6, -1),)}, (3, 4), 7, 2)
-X_ROW = ({0: ((3, 2), (1, 1), (2, -1))}, (), 0, 0)
-X_FIRST = ({0: ((1, 1), (2, -1))}, (1, 2), 3, 1)
-Z_SECOND = ({0: ((3, 2), (4, -2), (1, 1), (2, -1)), 3: ((5, 1),), 4: ((6, -1),)}, (3, 4), 7, 2)
+AG_SCHEMES = (
+    ({0: ((3, 2), (4, -2), (1, 1), (2, -1)), 3: ((5, 1),), 4: ((6, -1),)}, (3, 4), 7, 2),
+    ({0: ((3, 2), (1, 1), (2, -1))}, (), 0, 0),
+    ({0: ((1, 1), (2, -1))}, (1, 2), 3, 1),
+    ({0: ((3, 2), (4, -2), (1, 1), (2, -1)), 3: ((5, 1),), 4: ((6, -1),)}, (3, 4), 7, 2),
+)
+RS_SCHEMES = (
+    ({0: ((3, 2), (4, -2), (1, 1), (2, -1)), 3: ((5, 1),), 4: ((6, -1),)}, (3, 4), 7, 2),
+    ({0: ((3, 2), (1, 1), (2, -1))}, (), 0, 0),
+    ({0: ((1, 1), (2, -1))}, (1, 2), 3, 1),
+    ({0: ((3, 2), (4, -2), (1, 1), (2, -1)), 3: ((5, 1),), 4: ((6, -1),)}, (3, 4), 7, 2),
+)
 Z_REACH, X_REACH = ((1, 2), (1, 2))
-PARTS = ((1, 0, 96), (2, 96, 128))
+AG_PARTS = ((1, 0, 96), (2, 96, 128))
+RS_PARTS = ((1, 0, 96), (2, 96, 128))
 AG_ORDER = (
     (0,0,0,0), (0,0,0,1), (1,0,0), (0,0,3,0), (0,3,0,0), (0,4,0,0), (0,0,1,0), (0,0,2,0), (0,1,0,0), (0,0,3,1),
     (0,2,0,0), (1,0,3), (0,0,2,1), (0,0,1,1), (1,0,2), (1,0,1), (0,3,0,1), (0,4,0,1), (1,3,0), (1,4,0), (0,1,0,1),
-    (0,2,0,1), (1,1,0), (1,2,0), (0,3,1,0), (0,3,2,0), (2,(0,0),(0,3),(0,2),(0,1)), (0,5,0,0), (0,4,1,0), (0,4,2,0),
-    (2,(3,0),(4,0),(1,0),(2,0)), (0,7,0,0), (0,1,1,0), (0,1,2,0), (0,3,3,1), (0,6,0,0), (0,1,3,1), (0,2,1,0),
-    (0,2,2,0), (0,3,3,0), (1,3,3), (0,4,3,1), (0,3,2,1), (0,2,3,1), (1,3,2), (0,1,2,1), (1,1,2), (0,5,1,0), (0,5,2,0),
-    (0,4,2,1), (1,4,2), (0,4,3,0), (1,4,3), (0,3,1,1), (0,2,2,1), (1,3,1), (1,2,2), (0,1,1,1), (1,1,1), (0,5,0,1),
-    (1,5,0), (0,7,1,0), (0,7,2,0), (2,(3,3),(3,2),(1,2),(4,2)), (0,4,1,1), (1,4,1), (0,1,3,0), (0,2,1,1), (1,1,3),
-    (1,2,1), (2,(4,3),(3,1),(2,2),(1,1)), (0,7,0,1), (1,7,0), (0,6,1,0), (0,6,2,0), (0,5,3,1), (0,6,0,1), (1,6,0),
-    (0,2,3,0), (1,2,3), (0,7,3,1), (2,(5,0),(4,1),(1,3),(2,1)), (0,5,3,0), (1,5,3), (0,5,2,1), (0,6,3,1), (1,5,2),
-    (0,7,3,0), (1,7,3), (0,7,2,1), (1,7,2), (2,(7,0),(6,0),(2,3),(5,3)), (0,6,3,0), (0,5,1,1), (0,6,2,1), (1,6,3),
-    (1,5,1), (1,6,2), (0,7,1,1), (1,7,1), (0,6,1,1), (1,6,1), (2,(5,2),(7,3),(7,2),(6,3)), (2,(5,1),(6,2)),
-    (2,(7,1),(6,1)),
+    (0,2,0,1), (1,1,0), (1,2,0), (2,(0,0),(0,3)), (0,3,1,0), (0,3,2,0), (2,(0,2),(0,1)), (0,5,0,0), (2,(3,0),(4,0)),
+    (0,4,1,0), (0,4,2,0), (2,(1,0),(2,0)), (0,7,0,0), (0,1,1,0), (0,1,2,0), (0,3,3,1), (0,6,0,0), (0,1,3,1),
+    (0,2,1,0), (0,2,2,0), (0,3,3,0), (1,3,3), (0,4,3,1), (0,3,2,1), (0,2,3,1), (1,3,2), (0,1,2,1), (1,1,2), (0,5,1,0),
+    (0,5,2,0), (0,4,2,1), (1,4,2), (0,4,3,0), (1,4,3), (2,(3,3),(3,2)), (0,3,1,1), (0,2,2,1), (1,3,1), (1,2,2),
+    (0,1,1,1), (1,1,1), (0,5,0,1), (1,5,0), (0,7,1,0), (0,7,2,0), (2,(1,2),(4,2)), (0,4,1,1), (1,4,1), (0,1,3,0),
+    (0,2,1,1), (1,1,3), (1,2,1), (2,(4,3),(3,1)), (2,(2,2),(1,1)), (0,7,0,1), (1,7,0), (0,6,1,0), (0,6,2,0),
+    (0,5,3,1), (0,6,0,1), (1,6,0), (2,(5,0),(4,1)), (0,2,3,0), (1,2,3), (0,7,3,1), (2,(1,3),(2,1)), (0,5,3,0),
+    (1,5,3), (0,5,2,1), (0,6,3,1), (1,5,2), (0,7,3,0), (1,7,3), (2,(7,0),(6,0)), (0,7,2,1), (1,7,2), (2,(2,3),(5,3)),
+    (0,6,3,0), (0,5,1,1), (0,6,2,1), (1,6,3), (1,5,1), (1,6,2), (2,(5,2),(7,3)), (0,7,1,1), (1,7,1), (0,6,1,1),
+    (1,6,1), (2,(7,2),(6,3)), (2,(5,1),(6,2)), (2,(7,1),(6,1)),
 )
 RS_ORDER = (
-    (2,(7,3),(5,3),(6,3),(7,1)), (2,(7,2),(5,1),(6,1),(6,2)), (2,(5,2),(4,3),(3,3),(1,3)), (0,7,3,0), (0,7,3,1),
-    (0,5,3,0), (0,5,3,1), (0,6,3,0), (0,6,3,1), (2,(2,3),(7,0),(5,0),(6,0)), (0,7,1,1), (0,7,2,1), (0,5,1,1),
-    (2,(3,1),(4,1),(4,2),(3,2)), (0,6,1,1), (0,6,2,1), (0,5,2,1), (2,(2,1),(1,1),(2,2),(1,2)), (0,4,3,0), (0,3,3,0),
-    (0,1,3,0), (0,7,1,0), (0,7,2,0), (0,2,3,0), (0,7,0,1), (0,1,3,1), (0,5,1,0), (0,5,2,0), (0,3,3,1), (0,4,3,1),
-    (0,2,3,1), (0,6,1,0), (0,6,2,0), (0,5,0,1), (0,6,0,1), (2,(4,0),(3,0),(0,3),(1,0)), (0,2,1,1), (0,4,1,0),
-    (0,4,2,0), (0,1,1,1), (2,(2,0),(0,1),(0,2),(0,0)), (0,2,2,1), (0,3,1,0), (0,3,2,0), (0,1,2,1), (0,3,1,1),
-    (0,4,1,1), (0,1,1,0), (0,4,2,1), (0,3,2,1), (0,1,2,0), (0,0,3,0), (0,1,0,1), (0,2,0,1), (0,7,0,0), (0,0,1,0),
-    (0,2,1,0), (0,2,2,0), (0,0,2,0), (0,0,3,1), (0,5,0,0), (0,4,0,1), (0,3,0,1), (0,6,0,0), (0,0,1,1), (0,0,2,1),
-    (0,1,0,0), (0,3,0,0), (0,4,0,0), (0,2,0,0), (0,0,0,1), (0,0,0,0),
+    (2,(7,3),(5,3)), (2,(6,3),(7,1)), (2,(7,2),(5,1)), (2,(6,1),(6,2)), (2,(5,2),(4,3)), (2,(3,3),(1,3)), (0,7,3,0),
+    (0,7,3,1), (0,5,3,0), (0,5,3,1), (0,6,3,0), (0,6,3,1), (2,(2,3),(7,0)), (0,7,1,1), (0,7,2,1), (2,(5,0),(6,0)),
+    (0,5,1,1), (2,(3,1),(4,1)), (0,6,1,1), (0,6,2,1), (2,(4,2),(3,2)), (0,5,2,1), (2,(2,1),(1,1)), (0,4,3,0),
+    (0,3,3,0), (2,(2,2),(1,2)), (0,1,3,0), (0,7,1,0), (0,7,2,0), (0,2,3,0), (0,7,0,1), (0,1,3,1), (0,5,1,0),
+    (0,5,2,0), (0,3,3,1), (0,4,3,1), (0,2,3,1), (0,6,1,0), (0,6,2,0), (0,5,0,1), (0,6,0,1), (2,(4,0),(3,0)),
+    (2,(0,3),(1,0)), (0,2,1,1), (0,4,1,0), (0,4,2,0), (0,1,1,1), (2,(2,0),(0,1)), (0,2,2,1), (0,3,1,0), (0,3,2,0),
+    (0,1,2,1), (0,3,1,1), (0,4,1,1), (0,1,1,0), (0,4,2,1), (0,3,2,1), (0,1,2,0), (0,0,3,0), (0,1,0,1),
+    (2,(0,2),(0,0)), (0,2,0,1), (0,7,0,0), (0,0,1,0), (0,2,1,0), (0,2,2,0), (0,0,2,0), (0,0,3,1), (0,5,0,0),
+    (0,4,0,1), (0,3,0,1), (0,6,0,0), (0,0,1,1), (0,0,2,1), (0,1,0,0), (0,3,0,0), (0,4,0,0), (0,2,0,0), (0,0,0,1),
+    (0,0,0,0),
 )
-G_AT = (34, 64, 69, 71)
-
-
-def moves(kind, zi, xi):
+G_AT = (40, 72, 77, 79)
+
+
+def moves(schemes, kind, zi, xi):
+    z_column, x_row, x_first, z_second = schemes
     if kind == 1:
         if xi == 0:
-            yield "z", zi, Z_COLUMN
-        yield "x", xi, (X_FIRST if zi else X_ROW)
+            yield "z", zi, z_column
+        yield "x", xi, (x_first if zi else x_row)
     else:
         if zi == 0:
-            yield "x", xi, X_ROW
-        yield "z", zi, (Z_SECOND if xi else Z_COLUMN)
-
-
-def children(kind, zi, xi):
+            yield "x", xi, x_row
+        yield "z", zi, (z_second if xi else z_column)
+
+
+def children(schemes, kind, zi, xi):
     found = []
-    for axis, at, (steps, pair, last, hops) in moves(kind, zi, xi):
+    for axis, at, (steps, pair, last, hops) in moves(schemes, kind, zi, xi):
         for to, h in steps.get(at, ()):
             found.append((axis, (to, xi) if axis == "z" else (zi, to), h, None))
         if at in pair:
@@ -146,14 +157,14 @@
     seen = set()
 
     def ag_piece(zi, xi, p):
-        kind, r0, r1 = PARTS[p]
+        kind, r0, r1 = AG_PARTS[p]
         part = pl.ds(r0, r1 - r0)
         if (zi, xi) == (0, 0):
             source = features.at[part]
         else:
             source = gathered.at[zi, xi, 0, part]
             arrived(("ag", zi, xi, p), source)
-        for axis, (zd, xd), hops, pair in children(kind, zi, xi):
+        for axis, (zd, xd), hops, pair in children(AG_SCHEMES, kind, zi, xi):
             origin = source
             if pair is not None:
                 if (zd, xd, p) not in seen:
@@ -344,10 +355,10 @@
             send(("rss", back_batch[zi, xi]), "rs", sibsend.at[zi, xi], sibrecv.at[zi, xi], sibling)
 
     parent = {}
-    for p, (kind, _, _) in enumerate(PARTS):
+    for p, (kind, _, _) in enumerate(RS_PARTS):
         for zi in range(NZ):
             for xi in range(NX):
-                for axis, (zd, xd), hops, pair in children(kind, zi, xi):
+                for axis, (zd, xd), hops, pair in children(RS_SCHEMES, kind, zi, xi):
                     parent[zd, xd, p] = (axis, hops, pair)
 
     waited = set()
@@ -358,11 +369,11 @@
             arrived(name, dst)
 
     def rs_piece(zi, xi, p):
-        kind, r0, r1 = PARTS[p]
+        kind, r0, r1 = RS_PARTS[p]
         f = pl.ds(2 * r0, 2 * (r1 - r0))
         n = back_batch[zi, xi]
         once(("rss", n), sibrecv.at[pl.ds(0, back_size[n]), 0])
-        below = children(kind, zi, xi)
+        below = children(RS_SCHEMES, kind, zi, xi)
         for _, (zd, xd), _, _ in below:
             once(("rs", zd, xd, p), landed.at[zd, xd, f])
         total = own32[zi, xi, f] + sibrecv[zi, xi, f].astype(F32)
@@ -397,8 +408,22 @@
     sent("g7", g7.at[0])
 
 
-COPIES = 149
+COPIES = 164
 GROUPS = 8
+
+
+def hand_over(*refs):
+    count = 4
+    ins, outs, held, sems = refs[:count], refs[count:2 * count], refs[2 * count:3 * count], refs[-1]
+    first = [pltpu.make_async_copy(ins[n], held[n], sems.at[0, n]) for n in range(count)]
+    second = [pltpu.make_async_copy(held[n], outs[n], sems.at[1, n]) for n in range(count)]
+    for c in first:
+        c.start()
+    for c, d in zip(first, second):
+        c.wait()
+        d.start()
+    for d in second:
+        d.wait()
 
 
 def on_device(features, weight, bias, cotangent, tile_values, tile_rows, tile_cols, tile_count):
@@ -460,6 +485,16 @@
             transcendentals=node_rows * feat,
         ),
     )(features, weight, bias.reshape(1, feat), cotangent, tile_values, tile_rows, tile_cols, tile_count)
+    hbm = pl.BlockSpec(memory_space=pltpu.HBM)
+    results = (act, gf, gw, gb)
+    act, gf, gw, gb = pl.pallas_call(
+        hand_over,
+        out_shape=tuple(jax.ShapeDtypeStruct(a.shape, a.dtype) for a in results),
+        in_specs=[hbm] * 4,
+        out_specs=(hbm,) * 4,
+        scratch_shapes=[pltpu.VMEM(a.shape, a.dtype) for a in results] + [pltpu.SemaphoreType.DMA((2, 4))],
+        compiler_params=pltpu.CompilerParams(vmem_limit_bytes=64 * 1024 * 1024),
+    )(*results)
     return act, gf, gw, gb.reshape(feat)
 
 

time: 76.3 us -> 71.9 us (0.942)
  local copies, waits for them, and re-layouts: 5.81 us -> 0 us
  Pallas kernels: 69 us -> 70.5 us
    unnamed x4 -> x0, local copies, waits for them, and re-layouts: 5.81 us -> none
    pallas_call x0 -> x1, Pallas kernels: none -> 1.8 us  [on_device(): pl.pallas_call(hand_over, out_shape=tuple((jax.ShapeDtypeStruct(a.shape,...]
where the time goes in v3:
time: 71.9 us; the launch traced here: 71.8 us
  Pallas kernels  70.5 us (98%)
  between operations  1.29 us (2%)
    pallas_call x1, Pallas kernels, on_device(): pl.pallas_call(functools.partial(body, tile, slots, scale), out_shape=(ja...  68.7 us
    pallas_call x1, Pallas kernels, on_device(): pl.pallas_call(hand_over, out_shape=tuple((jax.ShapeDtypeStruct(a.shape,...  1.8 us

profile of v3, /device:TPU:1, one launch (start us, length us, event | category | flops | bytes accessed | tf_op | source)
XLA Modules:
  0.0 71.8 jit_solution(8259018042205385066)
XLA Ops:
  1.3 68.7 %shard_map.111 = (bf16[128,256]{1,0:T(8,128)(2,1)}, bf16[128,256]{1,0:T(8,128)(2,1)}, f32[256,256]{1,0:T(8,128)}, f32[1,256]{1,0:T(1,128)}) custom-call(bf16[128,256]{1,0:T(8,128)(2,1)} %features_hbm.1, bf16[256,256]{1,0:T(8,128)(2,1)} %weight_hbm.1, f32[1,256]{1,0:T(1,128)} %bitcast.2, bf16[128,256]{1,0:T(8,128)(2,1)} %cotangent_hbm.1, ...), custom_call_target="tpu_custom_call" | custom-call | flops 4294967296 | bytes 6291456 | tf_op jit(solution)/shard_map/pallas_call | solution.py:436
  70.0 1.8 %shard_map.112 = (bf16[128,256]{1,0:T(8,128)(2,1)}, bf16[128,256]{1,0:T(8,128)(2,1)}, f32[256,256]{1,0:T(8,128)}, f32[1,256]{1,0:T(1,128)}) custom-call(bf16[128,256]{1,0:T(8,128)(2,1)} %get-tuple-element.12.refs_0_, bf16[128,256]{1,0:T(8,128)(2,1)} %get-tuple-element.13.refs_1_, f32[256,256]{1,0:T(8,128)} %get-tuple-element.14.refs_2_, ...), custom_call_target="tpu_custom_call" | custom-call | tf_op jit(solution)/shard_map/pallas_call | solution.py:490

commit v4 on v3

--- a/solution.py
+++ b/solution.py
@@ -306,14 +306,19 @@
                 g2s[c, pl.ds(8, 8)] = total[half:half + 8]
             for dy, dx in square:
                 c, device = in_square(dy, dx)
-                send("g2", "g2", g2s.at[c], g2r.at[q], device)
+                n_rows = pl.ds(0, 16 if dy == 0 else 8)
+                send("g2", "g2", g2s.at[c, n_rows], g2r.at[q, n_rows], device)
             g2r[q] = g2s[q]
         elif n == 1:
-            arrived("g2", g2r.at[pl.ds(0, NY * NX - 1)])
-            total = g2r[0]
+            arrived("g2", g2r.at[pl.ds(0, 9)])
+            total = g2r[0, pl.ds(0, 8)]
             for c in range(1, NY * NX):
-                total = total + g2r[c]
-            g4r[z] = total
+                total = total + g2r[c, pl.ds(0, 8)]
+            g4r[z, pl.ds(0, 8)] = total
+            total = g2r[y * NX, pl.ds(8, 8)]
+            for c in range(1, NX):
+                total = total + g2r[y * NX + c, pl.ds(8, 8)]
+            g4r[z, pl.ds(8, 8)] = total
             for j in (4, 3, 5, 2, 6, 1, 7):
                 send("g4", "g4", g4r.at[z], g4r.at[z], z_off(j))
         elif n == 2:
@@ -321,14 +326,17 @@
             total = g4r[0]
             for j in range(1, NZ):
                 total = total + g4r[j]
-            total = total * scale
-            gb_out[...] = total[8:9]
-            g5[q] = total[0:8]
+            g5[q] = total * scale
             for dy, dx in square:
-                send("g5", "g5", g5.at[q], g5.at[q], in_square(dy, dx)[1])
+                n_rows = pl.ds(0, 16 if dx == 0 else 8)
+                send("g5", "g5", g5.at[q, n_rows], g5.at[q, n_rows], in_square(dy, dx)[1])
         elif n == 3:
-            arrived("g5", g5.at[pl.ds(0, NY * NX - 1)])
-            g7[k] = g5[...].reshape(half, feat)
+            arrived("g5", g5.at[pl.ds(0, 9)])
+            g7[k] = g5[:, pl.ds(0, 8)].reshape(half, feat)
+            total = g5[x, pl.ds(8, 8)]
+            for c in range(1, NY):
+                total = total + g5[c * NX + x, pl.ds(8, 8)]
+            gb_out[...] = total[0:1]
             send("g7", "g7", g7.at[k], g7.at[k], sibling)
         elif n == 4:
             arrived("g7", g7.at[1 - k])
@@ -402,9 +410,9 @@
     sent("yd", values.at[pl.ds(0, 4 * (NY - 1))])
     sent("rs", values.at[pl.ds(0, 2 * (2 * NZ * NX - 1))])
     sent("g1", g1r)
-    sent("g2", g2r.at[pl.ds(0, NY * NX - 1)])
+    sent("g2", g2r.at[pl.ds(0, 9)])
     sent("g4", g4r.at[pl.ds(0, NZ - 1)])
-    sent("g5", g5.at[pl.ds(0, NY * NX - 1)])
+    sent("g5", g5.at[pl.ds(0, 9)])
     sent("g7", g7.at[0])
 
 
@@ -470,7 +478,7 @@
             pltpu.VMEM((NY * NX, 16, feat), F32),
             pltpu.VMEM((NY * NX, 16, feat), F32),
             pltpu.VMEM((NZ, 16, feat), F32),
-            pltpu.VMEM((NY * NX, 8, feat), F32),
+            pltpu.VMEM((NY * NX, 16, feat), F32),
             pltpu.VMEM((2, half, feat), F32),
             pltpu.SemaphoreType.DMA((GROUPS,)),
             pltpu.SemaphoreType.DMA((COPIES,)),

time: 71.9 us -> 70.6 us (0.982)
  Pallas kernels: 70.5 us -> 69.2 us
    pallas_call x1, Pallas kernels: 68.7 us -> 67.4 us  [on_device(): pl.pallas_call(functools.partial(body, tile, slots, scale), out_shape=(ja...]
where the time goes in v4:
time: 70.6 us; the launch traced here: 70.5 us
  Pallas kernels  69.2 us (98%)
  between operations  1.29 us (2%)
    pallas_call x1, Pallas kernels, on_device(): pl.pallas_call(functools.partial(body, tile, slots, scale), out_shape=(ja...  67.4 us
    pallas_call x1, Pallas kernels, on_device(): pl.pallas_call(hand_over, out_shape=tuple((jax.ShapeDtypeStruct(a.shape,...  1.8 us

profile of v4, /device:TPU:1, one launch (start us, length us, event | category | flops | bytes accessed | tf_op | source)
XLA Modules:
  0.0 70.5 jit_solution(5265070525166921500)
XLA Ops:
  1.3 67.4 %shard_map.111 = (bf16[128,256]{1,0:T(8,128)(2,1)}, bf16[128,256]{1,0:T(8,128)(2,1)}, f32[256,256]{1,0:T(8,128)}, f32[1,256]{1,0:T(1,128)}) custom-call(bf16[128,256]{1,0:T(8,128)(2,1)} %features_hbm.1, bf16[256,256]{1,0:T(8,128)(2,1)} %weight_hbm.1, f32[1,256]{1,0:T(1,128)} %bitcast.2, bf16[128,256]{1,0:T(8,128)(2,1)} %cotangent_hbm.1, ...), custom_call_target="tpu_custom_call" | custom-call | flops 4294967296 | bytes 6291456 | tf_op jit(solution)/shard_map/pallas_call | solution.py:444
  68.7 1.8 %shard_map.112 = (bf16[128,256]{1,0:T(8,128)(2,1)}, bf16[128,256]{1,0:T(8,128)(2,1)}, f32[256,256]{1,0:T(8,128)}, f32[1,256]{1,0:T(1,128)}) custom-call(bf16[128,256]{1,0:T(8,128)(2,1)} %get-tuple-element.12.refs_0_, bf16[128,256]{1,0:T(8,128)(2,1)} %get-tuple-element.13.refs_1_, f32[256,256]{1,0:T(8,128)} %get-tuple-element.14.refs_2_, ...), custom_call_target="tpu_custom_call" | custom-call | tf_op jit(solution)/shard_map/pallas_call | solution.py:498

commit v5 on v4

--- a/solution.py
+++ b/solution.py
@@ -197,6 +197,17 @@
         xx = (x + sign * offset_of(xi) + NX) % NX
         return (zz * NX + xx) * 2 + k
 
+    def last_forward(chunks):
+        arrived(("share", batch_of[chunks[0]]), gathered.at[pl.ds(0, len(chunks)), 0, 1])
+        rhs = jnp.concatenate([gathered[zi, xi].reshape(2 * node_rows, feat) for zi, xi in chunks], axis=0)
+        for j in (2, 1, 3, 0):
+            lhs = jnp.concatenate([tile_pair((y + j) % NY, col_of(zi, xi, -1)) for zi, xi in chunks], axis=1)
+            total = acc[pl.ds(j * node_rows, node_rows)] + jnp.dot(lhs, rhs, preferred_element_type=F32)
+            if j == 0:
+                return total
+            ysend[j] = total.astype(BF16)
+            send("y", "yd", ysend.at[j], yrecv.at[j], y_off(j))
+
     def forward(chunks):
         arrived(("share", batch_of[chunks[0]]), gathered.at[pl.ds(0, len(chunks)), 0, 1])
         lhs = jnp.concatenate([
@@ -239,6 +250,7 @@
     values[slots] = jnp.zeros((tile, tile), BF16)
 
     ready = False
+    final = todo.pop()
     for what, *where in todo:
         if what == 0:
             ag_piece(*where)
@@ -252,10 +264,7 @@
                 ready = True
             forward(where)
 
-    for j in (2, 1, 3):
-        ysend[j] = acc[pl.ds(j * node_rows, node_rows)].astype(BF16)
-        send("y", "yd", ysend.at[j], yrecv.at[j], y_off(j))
-    agg = acc[pl.ds(0, node_rows)]
+    agg = last_forward(final[1:])
     arrived("y", yrecv.at[pl.ds(1, 3)])
     for j in (1, 3, 2):
         agg = agg + yrecv[j].astype(F32)

time: 70.6 us -> 70.9 us (level)
  no operation moved by 1% of the time
where the time goes in v5:
time: 70.9 us; the launch traced here: 70.8 us
  Pallas kernels  69.5 us (98%)
  between operations  1.29 us (2%)
    pallas_call x1, Pallas kernels, on_device(): pl.pallas_call(functools.partial(body, tile, slots, scale), out_shape=(ja...  67.7 us
    pallas_call x1, Pallas kernels, on_device(): pl.pallas_call(hand_over, out_shape=tuple((jax.ShapeDtypeStruct(a.shape,...  1.8 us

profile of v5, /device:TPU:1, one launch (start us, length us, event | category | flops | bytes accessed | tf_op | source)
XLA Modules:
  0.0 70.8 jit_solution(3159471359540151044)
XLA Ops:
  1.3 67.7 %shard_map.111 = (bf16[128,256]{1,0:T(8,128)(2,1)}, bf16[128,256]{1,0:T(8,128)(2,1)}, f32[256,256]{1,0:T(8,128)}, f32[1,256]{1,0:T(1,128)}) custom-call(bf16[128,256]{1,0:T(8,128)(2,1)} %features_hbm.1, bf16[256,256]{1,0:T(8,128)(2,1)} %weight_hbm.1, f32[1,256]{1,0:T(1,128)} %bitcast.2, bf16[128,256]{1,0:T(8,128)(2,1)} %cotangent_hbm.1, ...), custom_call_target="tpu_custom_call" | custom-call | flops 4294967296 | bytes 6291456 | tf_op jit(solution)/shard_map/pallas_call | solution.py:453
  69.0 1.8 %shard_map.112 = (bf16[128,256]{1,0:T(8,128)(2,1)}, bf16[128,256]{1,0:T(8,128)(2,1)}, f32[256,256]{1,0:T(8,128)}, f32[1,256]{1,0:T(1,128)}) custom-call(bf16[128,256]{1,0:T(8,128)(2,1)} %get-tuple-element.12.refs_0_, bf16[128,256]{1,0:T(8,128)(2,1)} %get-tuple-element.13.refs_1_, f32[256,256]{1,0:T(8,128)} %get-tuple-element.14.refs_2_, ...), custom_call_target="tpu_custom_call" | custom-call | tf_op jit(solution)/shard_map/pallas_call | solution.py:507
